TPU v7x, 128 devices: a whole 4x4x4 slice. The times are simulated.
128 devices in a mesh: replica: 2 (over z_lo), fsdp: 64 (over x, y, z_hi, core).
Axes of the slice: x: 4, y: 4, z: 4 (z_hi: 2, z_lo: 2; z = z_hi * 2 + z_lo), core: 2. Of those that a mesh axis runs over, the one named last changes fastest.
Arguments:
- inputs: bfloat16 [2, 2, 65536, 4096], P('replica', None, 'fsdp'), may hold values from -16 to 16
- targets: bfloat16 [2, 2, 65536, 512], P('replica', None, 'fsdp'), may hold values from -6 to 6
- weights: float32 [2, 4096, 512], P('replica', 'fsdp'), may hold values from -6 to 6
- first_moment: float32 [2, 4096, 512], P('replica', 'fsdp'), may hold values from -18 to 18
- second_moment: float32 [2, 4096, 512], P('replica', 'fsdp'), may hold values from 4 to 100
- global_weights: float32 [4096, 512], P('fsdp'), may hold values from -6 to 6
- outer_momentum: float32 [4096, 512], P('fsdp'), may hold values from -2 to 2
- outer_gradient: bfloat16 [2, 4096, 512], P('replica', 'fsdp'), may hold values from -2 to 2
- sync_step: int32 [1], replicated, may hold values from 0 to 1
Outputs:
- weights_out: float32 [2, 4096, 512], P('replica', 'fsdp')
- first_out: float32 [2, 4096, 512], P('replica', 'fsdp')
- second_out: float32 [2, 4096, 512], P('replica', 'fsdp')
- global_out: float32 [4096, 512], P('fsdp')
- momentum_out: float32 [4096, 512], P('fsdp')
Inputs may be any that keep to these rules, and one draw needn't show every extreme that they name: `sync_step`: the inner step after which each replica mixes in the new global weights; the same for both replicas.
All inputs are finite; a program needn't handle non-finite values.
Results may differ from a plain program's by a relative error of at most 0.008.
Values may be sent and summed in bfloat16 or wider, within the bound.
A program may use at most 256 MiB of HBM per device.

v0:
```python
import math

import jax
import jax.numpy as jnp
from jax import lax
from jax.sharding import PartitionSpec as P

D = 4096
STEPS = 2


def per_device(
    inputs,
    targets,
    weights,
    first_moment,
    second_moment,
    global_weights,
    outer_momentum,
    outer_gradient,
    sync_step,
):
    inv_root = 1.0 / math.sqrt(D)
    change = outer_gradient[0].astype(jnp.float32)
    replicas = lax.axis_size("replica")
    mean_change = lax.psum(change.astype(jnp.bfloat16), "replica").astype(jnp.float32) / replicas
    momentum_out = 0.9 * outer_momentum + mean_change
    global_out = global_weights - 0.7 * (mean_change + 0.9 * momentum_out)
    merge_step = sync_step[0]
    weight_now = weights[0]
    moment_one = first_moment[0]
    moment_two = second_moment[0]
    own_rows = weight_now.shape[0]
    for inner in range(STEPS):
        batch_rows = inputs[0, inner]
        weight_half = weight_now.astype(jnp.bfloat16)
        all_rows = lax.all_gather(weight_half, "fsdp", axis=0, tiled=True)
        product = jnp.dot(batch_rows, all_rows, preferred_element_type=jnp.float32)
        prediction = product * inv_root
        residual = (prediction - targets[0, inner].astype(jnp.float32)).astype(jnp.bfloat16)

        def grad_term(start, count, batch_rows=batch_rows, residual=residual):
            return lax.dot_general(
                batch_rows, residual, (((0,), (0,)), ((), ())), preferred_element_type=jnp.float32
            )

        gradient = (
            lax.psum_scatter(
                grad_term(jnp.int32(0), lax.axis_size("fsdp") * own_rows),
                "fsdp",
                scatter_dimension=0,
                tiled=True,
            )
            * inv_root
        )
        moment_one = 0.9 * moment_one + 0.1 * gradient
        moment_two = 0.95 * moment_two + 0.05 * gradient * gradient
        weight_now = weight_now - 0.05 * (
            moment_one / (jnp.sqrt(moment_two) + 1e-08) + 0.1 * weight_now
        )
        weight_now = jnp.where(merge_step == inner, 0.5 * weight_now + 0.5 * global_out, weight_now)
    return (weight_now[None], moment_one[None], moment_two[None], global_out, momentum_out)


def solution(mesh):
    in_specs = (
        P("replica", None, "fsdp", None),
        P("replica", None, "fsdp", None),
        P("replica", "fsdp", None),
        P("replica", "fsdp", None),
        P("replica", "fsdp", None),
        P("fsdp", None),
        P("fsdp", None),
        P("replica", "fsdp", None),
        P(),
    )
    out_specs = (
        P("replica", "fsdp", None),
        P("replica", "fsdp", None),
        P("replica", "fsdp", None),
        P("fsdp", None),
        P("fsdp", None),
    )
    return jax.shard_map(
        per_device, mesh=mesh, in_specs=in_specs, out_specs=out_specs, check_vma=False
    )
```

profile of v0, /device:TPU:1, one launch (start us, length us, event | category | flops | bytes accessed | tf_op | source)
XLA Modules:
  0.0 906.5 jit_solution(3787205557622586890)
XLA Ops:
  8.0 0.0 all-gather.3.cloned.1.call-start
  8.0 1.5 bitcast_convert_fusion
  9.6 0.0 all-gather.3.cloned.1.call-update
  9.6 0.0 all-reduce.2.cloned.1.call-start
  9.7 0.5 all-reduce.2.cloned.1.call-update
  10.2 0.0 reduce-scatter.7.cloned.1.call-start
  10.2 79.2 %all-gather.3.cloned.1.call-done = bf16[4096,512]{1,0:T(8,128)(2,1)} async-done(((bf16[64,512]{1,0:T(8,128)(2,1)}), bf16[4096,512]{1,0:T(8,128)(2,1)}) %all-gather.3.cloned.1.call-update) | async-done | bytes 4194320 | tf_op jit(solution)/shard_map/all_gather | solution.py:37
  89.4 19.5 %fusion.12 = f32[4096,512]{0,1:T(8,128)} fusion(bf16[1,2,1024,4096]{3,2,1,0:T(8,128)(2,1)} %param.9, bf16[4096,512]{1,0:T(8,128)(2,1)} %all-gather.3.cloned.1.call-done, bf16[1,2,1024,512]{3,2,1,0:T(8,128)(2,1)} %param.10), kind=kOutput, calls=%fused_computation.12 | convolution fusion | flops 8592031744 | bytes 30408704 | tf_op jit(solution)/shard_map/dot_general | solution.py:43
  108.9 9.0 copy.31
  117.9 0.0 copy-start.6
  118.0 0.0 copy-start.7
  118.0 0.0 reduce-scatter.7.cloned.1.call-update
  118.0 0.0 all-gather.5.cloned.1.call-start
  118.8 0.0 all-reduce.2.cloned.1.call-done
  118.9 335.2 %reduce-scatter.7.cloned.1.call-done = f32[64,512]{1,0:T(8,128)} async-done(((f32[4096,512]{1,0:T(8,128)}), f32[64,512]{1,0:T(8,128)}) %reduce-scatter.7.cloned.1.call-update) | async-done | bytes 131088 | tf_op jit(solution)/shard_map/reduce_scatter | solution.py:48
  454.1 0.0 copy-done
  454.1 0.0 copy-done.1
  454.1 0.0 copy-done.2
  454.1 0.0 copy-done.5
  454.1 0.0 copy-done.6
  454.1 1.7 fusion.40
  455.8 0.0 all-gather.5.cloned.1.call-update
  455.9 0.2 reduce-scatter.9.cloned.1.call-start
  456.1 76.5 %all-gather.5.cloned.1.call-done = bf16[4096,512]{1,0:T(8,128)(2,1)} async-done(((bf16[64,512]{1,0:T(8,128)(2,1)}), bf16[4096,512]{1,0:T(8,128)(2,1)}) %all-gather.5.cloned.1.call-update) | async-done | bytes 4194320 | tf_op jit(solution)/shard_map/all_gather | solution.py:37
  532.6 0.0 copy-done.7
  532.6 19.2 %fusion.15 = f32[4096,512]{0,1:T(8,128)} fusion(bf16[1,2,1024,4096]{3,2,1,0:T(8,128)(2,1)} %param.9, bf16[4096,512]{1,0:T(8,128)(2,1)} %all-gather.5.cloned.1.call-done, bf16[1,2,1024,512]{3,2,1,0:T(8,128)(2,1)S(1)} %copy-done.7), kind=kOutput, calls=%fused_computation.13 | convolution fusion | flops 8592031744 | bytes 30408704 | tf_op jit(solution)/shard_map/dot_general | solution.py:43
  551.8 9.0 copy.33
  560.8 0.0 reduce-scatter.9.cloned.1.call-update
  560.8 336.6 %reduce-scatter.9.cloned.1.call-done = f32[64,512]{1,0:T(8,128)} async-done(((f32[4096,512]{1,0:T(8,128)}), f32[64,512]{1,0:T(8,128)}) %reduce-scatter.9.cloned.1.call-update) | async-done | bytes 131088 | tf_op jit(solution)/shard_map/reduce_scatter | solution.py:48
  897.5 0.0 copy-done.4
  897.5 0.0 copy-done.3
  897.5 1.9 fusion.37
  (6 shorter events, 0.0 us)
Async XLA Ops:
  8.0 81.4 %all-gather.3.cloned.1.call-start = ((), (), s32[]{:S(2)}) async-start(), calls=%async_computation.2 | async-start | bytes 4259840 | tf_op jit(solution)/shard_map/all_gather | solution.py:37
  9.6 109.3 %all-reduce.2.cloned.1.call-start = ((), (), s32[]{:S(2)}) async-start(), calls=%async_computation.3 | async-start | bytes 131072 | tf_op jit(solution)/shard_map/psum | solution.py:26
  10.2 443.9 %reduce-scatter.7.cloned.1.call-start = ((), (), s32[]{:S(2)}) async-start(), calls=%async_computation.5 | async-start | bytes 8519680 | tf_op jit(solution)/shard_map/reduce_scatter | solution.py:48
  117.9 336.2 %copy-start = (f32[1,64,512]{2,1,0:T(8,128)S(1)}, f32[1,64,512]{2,1,0:T(8,128)}, u32[]{:S(2)}) copy-start(f32[1,64,512]{2,1,0:T(8,128)} %param.11) | copy-start | bytes 393220
  117.9 336.2 %copy-start.1 = (f32[1,64,512]{2,1,0:T(8,128)S(1)}, f32[1,64,512]{2,1,0:T(8,128)}, u32[]{:S(2)}) copy-start(f32[1,64,512]{2,1,0:T(8,128)} %param.12) | copy-start | bytes 393220
  117.9 336.2 %copy-start.2 = (f32[1,64,512]{2,1,0:T(8,128)S(1)}, f32[1,64,512]{2,1,0:T(8,128)}, u32[]{:S(2)}) copy-start(f32[1,64,512]{2,1,0:T(8,128)} %param.13) | copy-start | bytes 393220
  117.9 336.2 %copy-start.5 = (f32[64,512]{1,0:T(8,128)S(1)}, f32[64,512]{1,0:T(8,128)}, u32[]{:S(2)}) copy-start(f32[64,512]{1,0:T(8,128)} %param.14) | copy-start | bytes 393220
  117.9 336.2 %copy-start.6 = (f32[64,512]{1,0:T(8,128)S(1)}, f32[64,512]{1,0:T(8,128)}, u32[]{:S(2)}) copy-start(f32[64,512]{1,0:T(8,128)} %param.15) | copy-start | bytes 393220
  118.0 414.6 %copy-start.7 = (bf16[1,2,1024,512]{3,2,1,0:T(8,128)(2,1)S(1)}, bf16[1,2,1024,512]{3,2,1,0:T(8,128)(2,1)}, u32[]{:S(2)}) copy-start(bf16[1,2,1024,512]{3,2,1,0:T(8,128)(2,1)} %param.10) | copy-start | bytes 6291460
  118.0 414.6 %all-gather.5.cloned.1.call-start = ((), (), s32[]{:S(2)}) async-start(), calls=%async_computation.4 | async-start | bytes 4259840 | tf_op jit(solution)/shard_map/all_gather | solution.py:37
  455.8 441.6 %copy-start.4 = (f32[64,512]{1,0:T(8,128)}, f32[64,512]{1,0:T(8,128)S(1)}, u32[]{:S(2)}) copy-start(f32[64,512]{1,0:T(8,128)S(1)} %get-tuple-element.11) | copy-start | bytes 393220
  455.9 441.6 %reduce-scatter.9.cloned.1.call-start = ((), (), s32[]{:S(2)}) async-start(), calls=%async_computation.6 | async-start | bytes 8519680 | tf_op jit(solution)/shard_map/reduce_scatter | solution.py:48
  560.8 336.7 %copy-start.3 = (f32[64,512]{1,0:T(8,128)S(1)}, f32[64,512]{1,0:T(8,128)}, u32[]{:S(2)}) copy-start(f32[64,512]{1,0:T(8,128)} %reduce-scatter.7.cloned.1.call-done) | copy-start | bytes 393220
Sparse Core Ops, SparseCore 0:
  12.4 76.9 all-gather.2
  118.1 335.9 reduce-scatter.6
  457.7 74.8 all-gather.4
  561.0 336.4 reduce-scatter.8
Sparse Core Ops, SparseCore 1:
  12.5 30.1 all-reduce.1
where the time goes:
time: 914 us; the launch traced here: 906 us
  waiting for transfers between devices  828 us (91%)
  matrix products  38.6 us (4%)
  local copies, waits for them, and re-layouts  18.1 us (2%)
  between operations  16.1 us (2%)
    reduce_scatter x2, waiting for transfers between devices, per_device(): lax.psum_scatter(grad_term(jnp.int32(0), lax.axis_size('fsdp') * own_rows...  672 us
    all_gather x2, waiting for transfers between devices, per_device(): all_rows = lax.all_gather(weight_half, 'fsdp', axis=0, tiled=True)  156 us
    dot_general x2, matrix products, grad_term(): lax.dot_general(batch_rows, residual, (((0,), (0,)), ((), ())), preferred...  38.6 us
  transfers between devices with their start and end apart: 5, of which 4 were waited for; matrix products, arithmetic and copies ran while one was open for 3% of the time, Pallas kernels for 0%

commit v1 on v0

v1 whole, which is shorter than its diff:
```python
import functools
import math

import jax
import jax.numpy as jnp
from jax import lax
from jax.experimental import pallas as pl
from jax.experimental.pallas import tpu as pltpu
from jax.sharding import PartitionSpec as P

D = 4096
KVW = 512
STEPS = 2
NX, NY, NZ = 4, 4, 2
LOCAL = 1024
TOK = 2 * LOCAL
COLS = KVW // 2
ROWS = 128
HALF = ROWS // 2
CH = COLS // 2
MESH = pl.DeviceIdType.MESH
F32 = jnp.float32
BF16 = jnp.bfloat16

GROUPS = (
    (((0, 2), (1, 2), (2, 2), (3, 2)), (0, 2)),
    (((2, 0), (2, 1), (2, 3)), (1, 2)),
    (((0, 1), (1, 1), (3, 1)), (0, 1)),
    (((1, 0), (1, 3)), (1, 1)),
    (((0, 3), (3, 3)), (0, 3)),
    (((3, 0),), (1, 3)),
    (((0, 0),), None),
)


def dot(a, b):
    return lax.dot_general(a, b, (((1,), (0,)), ((), ())), preferred_element_type=F32)


def kernel(
    x_in,
    t_in,
    w_in,
    m_in,
    v_in,
    gw_in,
    om_in,
    og_in,
    sync_in,
    w_out,
    m_out,
    v_out,
    g_out,
    mo_out,
    xv,
    tv,
    wv,
    mv,
    vv,
    gv,
    gl,
    og,
    wg,
    rt,
    gb,
    r2,
    s1,
    r1,
    loc_sem,
    pre_send,
    pre_recv,
    x_loc,
    x_send,
    x_recv,
    a1_send,
    a1_recv,
    a2_send,
    a2_recv,
    r2_send,
    r2_recv,
    r1_send,
    r1_recv,
    out_loc,
    out_send,
    out_recv,
):
    inv_root = 1.0 / math.sqrt(D)
    rep = lax.axis_index("replica")
    me = lax.axis_index("fsdp")
    c = lax.rem(me, 2)
    zh = lax.rem(lax.div(me, 2), 2)
    y = lax.rem(lax.div(me, 4), 4)
    x = lax.div(me, 16)

    def dev(dx, dy, dz):
        nx, ny = lax.rem(x + dx, 4), lax.rem(y + dy, 4)
        nz = 1 - zh if dz else zh
        return (rep, ((nx * 4 + ny) * 2 + nz) * 2 + c)

    sibling = (rep, me + 1 - 2 * c)
    partner = (1 - rep, me)
    cols = pl.ds(pl.multiple_of(c * COLS, COLS), COLS)
    cols_o = pl.ds(pl.multiple_of((1 - c) * COLS, COLS), COLS)
    rows = pl.ds(pl.multiple_of(c * HALF, HALF), HALF)
    rows_o = pl.ds(pl.multiple_of((1 - c) * HALF, HALF), HALF)

    def remote(src, dst, send, recv, where):
        return pltpu.make_async_remote_copy(
            src_ref=src, dst_ref=dst, send_sem=send, recv_sem=recv, device_id=where, device_id_type=MESH
        )

    local = [
        pltpu.make_async_copy(w_in.at[0, :, cols], wv.at[rows], loc_sem.at[0]),
        pltpu.make_async_copy(m_in.at[0, :, cols], mv.at[rows], loc_sem.at[1]),
        pltpu.make_async_copy(v_in.at[0, :, cols], vv.at[rows], loc_sem.at[2]),
        pltpu.make_async_copy(gw_in, gl.at[0], loc_sem.at[3]),
        pltpu.make_async_copy(om_in, gl.at[1], loc_sem.at[4]),
        pltpu.make_async_copy(og_in.at[0], og.at[0], loc_sem.at[5]),
    ]
    for copy in local:
        copy.start()

    barrier = pltpu.get_barrier_semaphore()
    peers = [(dx, 0, dz) for dx in range(4) for dz in range(2) if dx or dz]
    peers += [(0, dy, dz) for dy in range(1, 4) for dz in range(2)]
    partners = [dev(*p) for p in peers] + [sibling, partner]
    for where in partners:
        pl.semaphore_signal(barrier, inc=1, device_id=where, device_id_type=MESH)
    pl.semaphore_wait(barrier, len(partners))

    pre = [
        remote(w_in.at[0, :, cols_o], wv.at[rows], pre_send.at[0], pre_recv.at[0], sibling),
        remote(m_in.at[0, :, cols_o], mv.at[rows], pre_send.at[1], pre_recv.at[1], sibling),
        remote(v_in.at[0, :, cols_o], vv.at[rows], pre_send.at[2], pre_recv.at[2], sibling),
        remote(og_in.at[0], og.at[1], pre_send.at[3], pre_recv.at[3], partner),
    ]
    for copy in pre:
        copy.start()

    def x_copies(step):
        own = pl.ds(0, LOCAL)
        other = pl.ds(LOCAL, LOCAL)
        return [
            pltpu.make_async_copy(x_in.at[0, step], xv.at[step, own], x_loc.at[step, 0]),
            pltpu.make_async_copy(t_in.at[0, step, :, cols], tv.at[step, own], x_loc.at[step, 1]),
            remote(x_in.at[0, step], xv.at[step, other], x_send.at[step, 0], x_recv.at[step, 0], sibling),
            remote(t_in.at[0, step, :, cols_o], tv.at[step, other], x_send.at[step, 1], x_recv.at[step, 1], sibling),
        ]

    for copy in x_copies(0):
        copy.start()
    local[0].wait()
    pre[0].wait_recv()

    def own_rows(kind):
        return slice(0, HALF) if kind == 0 else slice(HALF, ROWS)

    def delta(kind, along, dz):
        return (along, 0, dz) if kind == 0 else (0, along, dz)

    def long_delta(kind, along):
        return (0, along, 0) if kind == 0 else (along, 0, 0)

    def slot(along, dz):
        return dz * 4 + along

    def back(along):
        return (4 - along) % 4

    def gather_one(kind, along, dz):
        piece = wg.at[x, y, zh, own_rows(kind)]
        return remote(
            piece,
            piece,
            a1_send.at[kind, slot(along, dz)],
            a1_recv.at[kind, slot(back(along), dz)],
            dev(*delta(kind, along, dz)),
        )

    def gather_two(kind, plane, along):
        nz = 1 - zh if plane else zh
        lane = wg.at[:, y, nz, own_rows(kind)] if kind == 0 else wg.at[x, :, nz, own_rows(kind)]
        return remote(
            lane,
            lane,
            a2_send.at[kind, plane, along],
            a2_recv.at[kind, plane, back(along)],
            dev(*long_delta(kind, along)),
        )

    def arrived(copy_of, *args):
        copy_of(*args).wait_recv()

    def scatter_two(kind, along):
        if kind == 0:
            src = gb.at[:, lax.rem(y + along, 4), :, 0:CH]
        else:
            src = gb.at[lax.rem(x + along, 4), :, :, CH:COLS]
        return remote(
            src,
            r2.at[kind, back(along) - 1],
            r2_send.at[kind, along],
            r2_recv.at[kind, back(along)],
            dev(*long_delta(kind, along)),
        )

    def scatter_one(kind, along, dz):
        return remote(
            s1.at[kind, slot(along, dz)],
            r1.at[kind, slot(back(along), dz)],
            r1_send.at[kind, slot(along, dz)],
            r1_recv.at[kind, slot(back(along), dz)],
            dev(*delta(kind, along, dz)),
        )

    short = [(along, dz) for dz in range(2) for along in (2, 1, 3, 0) if along or dz]

    def inner(step, carry):
        wg[x, y, zh] = wv[...].astype(BF16)
        for along, dz in short:
            for kind in range(2):
                gather_one(kind, along, dz).start()

        @pl.when(step == 0)
        def outer():
            for copy in local[1:]:
                copy.wait()
            for copy in pre[1:]:
                copy.wait_recv()
            mean = (og[0].astype(F32) + og[1].astype(F32)) / 2.0
            momentum = 0.9 * gl[1] + mean
            gl[1] = momentum
            gl[0] = gl[0] - 0.7 * (mean + 0.9 * momentum)
            here = pltpu.make_async_copy(gl.at[0, :, cols], gv.at[rows], loc_sem.at[6])
            there = remote(gl.at[0, :, cols_o], gv.at[rows], pre_send.at[4], pre_recv.at[4], sibling)
            outs = [
                pltpu.make_async_copy(gl.at[0], g_out, out_loc.at[3]),
                pltpu.make_async_copy(gl.at[1], mo_out, out_loc.at[4]),
            ]
            for copy in [here, there] + outs:
                copy.start()
            here.wait()
            there.wait()
            for copy in outs:
                copy.wait()
            for copy in pre:
                copy.wait_send()

        for plane in range(2):
            for kind in range(2):
                for along, dz in short:
                    if dz == plane:
                        arrived(gather_one, kind, along, dz)
                for along in (2, 1, 3):
                    gather_two(kind, plane, along).start()
        for kind in range(2):
            for plane in range(2):
                for along in (2, 1, 3):
                    arrived(gather_two, kind, plane, along)
        for copy in x_copies(step):
            copy.wait()

        @pl.when(step == 0)
        def more():
            for copy in x_copies(1):
                copy.start()

        def forward(i, carry):
            block = pl.ds(pl.multiple_of(i * 512, 512), 512)
            product = dot(xv[step, block, :], wg[...].reshape(D, COLS))
            residual = product * inv_root - tv[step, block, :].astype(F32)
            rt[:, block] = residual.astype(BF16).T
            return carry

        lax.fori_loop(0, TOK // 512, forward, 0)

        for kind in range(2):
            for along, dz in short:
                gather_one(kind, along, dz).wait_send()
            for plane in range(2):
                for along in (2, 1, 3):
                    gather_two(kind, plane, along).wait_send()

        for tiles, send in GROUPS:
            for dx, dy in tiles:
                nx, ny = lax.rem(x + dx, 4), lax.rem(y + dy, 4)
                lanes = pl.ds(pl.multiple_of((nx * 4 + ny) * 256, 256), 256)
                tile = dot(rt[...], xv[step, :, lanes]).astype(BF16)
                gb[nx, ny, 0] = tile[:, :ROWS]
                gb[nx, ny, 1] = tile[:, ROWS:]
            if send is not None:
                scatter_two(*send).start()

        for kind in range(2):
            for along in (2, 1, 3):
                arrived(scatter_two, kind, along)
            mine = slice(0, CH) if kind == 0 else slice(CH, COLS)
            for along, dz in [(0, 0)] + short:
                nz = 1 - zh if dz else zh
                far = lax.rem((x if kind == 0 else y) + along, 4)
                here = gb[far, y, nz, mine] if kind == 0 else gb[x, far, nz, mine]
                total = here.astype(F32)
                for source in range(3):
                    total += r2[kind, source, far, nz].astype(F32)
                if along or dz:
                    s1[kind, slot(along, dz)] = total.astype(BF16)
                    scatter_one(kind, along, dz).start()
                else:
                    keep = total
            if kind == 0:
                keep_a = keep
            else:
                keep_b = keep

        halves = []
        for kind, total in ((0, keep_a), (1, keep_b)):
            for along, dz in short:
                arrived(scatter_one, kind, along, dz)
                total += r1[kind, slot(back(along), dz)].astype(F32)
            halves.append(total)
        gradient = jnp.concatenate(halves, axis=0).T * inv_root
        first = 0.9 * mv[...] + 0.1 * gradient
        second = 0.95 * vv[...] + 0.05 * gradient * gradient
        weight = wv[...]
        weight = weight - 0.05 * (first / (jnp.sqrt(second) + 1e-08) + 0.1 * weight)
        weight = jnp.where(sync_in[0] == step, 0.5 * weight + 0.5 * gv[...], weight)
        mv[...] = first
        vv[...] = second
        wv[...] = weight

        for kind in range(2):
            for along in (2, 1, 3):
                scatter_two(kind, along).wait_send()
            for along, dz in short:
                scatter_one(kind, along, dz).wait_send()
        return carry

    lax.fori_loop(0, STEPS, inner, 0)

    ends = []
    for i, (value, out) in enumerate(((wv, w_out), (mv, m_out), (vv, v_out))):
        ends.append(remote(value.at[rows_o], out.at[0, :, cols], out_send.at[i], out_recv.at[i], sibling))
        ends.append(pltpu.make_async_copy(value.at[rows], out.at[0, :, cols], out_loc.at[i]))
    for copy in ends:
        copy.start()
    for copy in ends:
        copy.wait()


def per_device(*args):
    shapes = ((1, 64, KVW),) * 3 + ((64, KVW),) * 2
    dma = pltpu.SemaphoreType.DMA
    anywhere = pl.BlockSpec(memory_space=pl.ANY)
    return pl.pallas_call(
        kernel,
        out_shape=tuple(jax.ShapeDtypeStruct(s, F32) for s in shapes),
        in_specs=[anywhere] * 8 + [pl.BlockSpec(memory_space=pltpu.SMEM)],
        out_specs=(anywhere,) * 5,
        scratch_shapes=[
            pltpu.VMEM((STEPS, TOK, D), BF16),
            pltpu.VMEM((STEPS, TOK, COLS), BF16),
            pltpu.VMEM((ROWS, COLS), F32),
            pltpu.VMEM((ROWS, COLS), F32),
            pltpu.VMEM((ROWS, COLS), F32),
            pltpu.VMEM((ROWS, COLS), F32),
            pltpu.VMEM((2, HALF, KVW), F32),
            pltpu.VMEM((2, HALF, KVW), BF16),
            pltpu.VMEM((NX, NY, NZ, ROWS, COLS), BF16),
            pltpu.VMEM((COLS, TOK), BF16),
            pltpu.VMEM((NX, NY, NZ, COLS, ROWS), BF16),
            pltpu.VMEM((2, 3, 4, NZ, CH, ROWS), BF16),
            pltpu.VMEM((2, 8, CH, ROWS), BF16),
            pltpu.VMEM((2, 8, CH, ROWS), BF16),
            dma((7,)),
            dma((5,)),
            dma((5,)),
            dma((STEPS, 2)),
            dma((STEPS, 2)),
            dma((STEPS, 2)),
            dma((2, 8)),
            dma((2, 8)),
            dma((2, 2, 4)),
            dma((2, 2, 4)),
            dma((2, 4)),
            dma((2, 4)),
            dma((2, 8)),
            dma((2, 8)),
            dma((5,)),
            dma((3,)),
            dma((3,)),
        ],
        compiler_params=pltpu.CompilerParams(
            collective_id=0, has_side_effects=True, vmem_limit_bytes=60 * 1024 * 1024
        ),
    )(*args)


def solution(mesh):
    in_specs = (
        P("replica", None, "fsdp", None),
        P("replica", None, "fsdp", None),
        P("replica", "fsdp", None),
        P("replica", "fsdp", None),
        P("replica", "fsdp", None),
        P("fsdp", None),
        P("fsdp", None),
        P("replica", "fsdp", None),
        P(),
    )
    out_specs = (
        P("replica", "fsdp", None),
        P("replica", "fsdp", None),
        P("replica", "fsdp", None),
        P("fsdp", None),
        P("fsdp", None),
    )
    return jax.shard_map(
        per_device, mesh=mesh, in_specs=in_specs, out_specs=out_specs, check_vma=False
    )
```

time: 914 us -> 123 us (0.13)
  waiting for transfers between devices: 828 us -> 0 us
  Pallas kernels: 0 us -> 113 us
  matrix products: 38.6 us -> 0 us
  between operations: 16.1 us -> 1.29 us
  local copies, waits for them, and re-layouts: 18.1 us -> 7.84 us
    reduce_scatter x2 -> x0, waiting for transfers between devices: 672 us -> none  [per_device(): lax.psum_scatter(grad_term(jnp.int32(0), lax.axis_size('fsdp') * own_rows...]
    all_gather x2 -> x0, waiting for transfers between devices: 156 us -> none  [per_device(): all_rows = lax.all_gather(weight_half, 'fsdp', axis=0, tiled=True)]
    pallas_call x0 -> x1, Pallas kernels: none -> 113 us  [per_device(): pl.pallas_call(kernel, out_shape=tuple((jax.ShapeDtypeStruct(s, F32) for...]
    dot_general x2 -> x0, matrix products: 38.6 us -> none  [grad_term(): lax.dot_general(batch_rows, residual, (((0,), (0,)), ((), ())), preferred...]
    unnamed x18 -> x5, local copies, waits for them, and re-layouts: 18.1 us -> 7.84 us
  transfers between devices with their start and end apart: 5 -> 0, of which waited for: 4 -> 0; matrix products, arithmetic and copies ran while one was open for 3% -> 0% of each run, Pallas kernels for 0% -> 0%
where the time goes in v1:
time: 123 us
  Pallas kernels  113 us (92%)
  local copies, waits for them, and re-layouts  7.84 us (6%)
  between operations  1.29 us (1%)
    pallas_call x1, Pallas kernels, per_device(): pl.pallas_call(kernel, out_shape=tuple((jax.ShapeDtypeStruct(s, F32) for...  113 us
    unnamed x5, local copies, waits for them, and re-layouts  7.84 us

profile of v1, /device:TPU:1, one launch (start us, length us, event | category | flops | bytes accessed | tf_op | source)
XLA Modules:
  0.0 122.6 jit_solution(3652001874842688778)
XLA Ops:
  1.3 113.5 %shard_map.128 = (f32[1,64,512]{2,1,0:T(8,128)}, f32[1,64,512]{2,1,0:T(8,128)}, f32[1,64,512]{2,1,0:T(8,128)}, f32[64,512]{1,0:T(8,128)}, f32[64,512]{1,0:T(8,128)}) custom-call(bf16[1,2,1024,4096]{3,2,1,0:T(8,128)(2,1)} %x_in.1, bf16[1,2,1024,512]{3,2,1,0:T(8,128)(2,1)} %t_in.1, f32[1,64,512]{2,1,0:T(8,128)} %w_in.1, f32[1,64,512]{2,1,0:T(8,128)} %m_in.1, ...), custom_call_target="tpu_custom_call" | custom-call | tf_op jit(solution)/shard_map/pallas_call | solution.py:354
  114.8 1.6 %copy.20 = f32[1,64,512]{2,1,0:T(8,128)} copy(f32[1,64,512]{2,1,0:T(8,128)} %get-tuple-element.10) | data formatting | bytes 262144
  116.3 1.6 %copy.21 = f32[1,64,512]{2,1,0:T(8,128)} copy(f32[1,64,512]{2,1,0:T(8,128)} %get-tuple-element.11) | data formatting | bytes 262144
  117.9 1.6 %copy.22 = f32[1,64,512]{2,1,0:T(8,128)} copy(f32[1,64,512]{2,1,0:T(8,128)} %get-tuple-element.12) | data formatting | bytes 262144
  119.5 1.6 %copy.23 = f32[64,512]{1,0:T(8,128)} copy(f32[64,512]{1,0:T(8,128)} %get-tuple-element.13) | data formatting | bytes 262144
  121.0 1.6 %copy.24 = f32[64,512]{1,0:T(8,128)} copy(f32[64,512]{1,0:T(8,128)} %get-tuple-element.14) | data formatting | bytes 262144

commit v2 on v1

v2 whole, which is shorter than its diff:
```python
import functools
import math

import jax
import jax.numpy as jnp
from jax import lax
from jax.experimental import pallas as pl
from jax.experimental.pallas import tpu as pltpu
from jax.sharding import PartitionSpec as P

D = 4096
KVW = 512
STEPS = 2
NX, NY, NZ = 4, 4, 2
LOCAL = 1024
TOK = 2 * LOCAL
COLS = KVW // 2
ROWS = 128
HALF = ROWS // 2
CHUNKS = 2
CK = COLS // CHUNKS
CH = CK // 2
MESH = pl.DeviceIdType.MESH
F32 = jnp.float32
BF16 = jnp.bfloat16

GROUPS = (
    (((0, 2), (1, 2), (2, 2), (3, 2)), (0, 2)),
    (((2, 0), (2, 1), (2, 3)), (1, 2)),
    (((0, 1), (1, 1), (3, 1)), (0, 1)),
    (((1, 0), (1, 3)), (1, 1)),
    (((0, 3), (3, 3)), (0, 3)),
    (((3, 0),), (1, 3)),
    (((0, 0),), None),
)


def dot(a, b):
    return lax.dot_general(a, b, (((1,), (0,)), ((), ())), preferred_element_type=F32)


def kernel(
    x_in,
    t_in,
    w_in,
    m_in,
    v_in,
    gw_in,
    om_in,
    og_in,
    sync_in,
    w_out,
    m_out,
    v_out,
    g_out,
    mo_out,
    xv,
    tv,
    wv,
    mv,
    vv,
    gv,
    gl,
    og,
    wg,
    rt,
    gb,
    r2,
    s1,
    r1,
    kept,
    loc_sem,
    pre_send,
    pre_recv,
    x_loc,
    x_send,
    x_recv,
    a1_send,
    a1_recv,
    a2_send,
    a2_recv,
    r2_send,
    r2_recv,
    r1_send,
    r1_recv,
    out_loc,
    out_send,
    out_recv,
):
    inv_root = 1.0 / math.sqrt(D)
    rep = lax.axis_index("replica")
    me = lax.axis_index("fsdp")
    c = lax.rem(me, 2)
    zh = lax.rem(lax.div(me, 2), 2)
    y = lax.rem(lax.div(me, 4), 4)
    x = lax.div(me, 16)

    def dev(dx, dy, dz):
        nx, ny = lax.rem(x + dx, 4), lax.rem(y + dy, 4)
        nz = 1 - zh if dz else zh
        return (rep, ((nx * 4 + ny) * 2 + nz) * 2 + c)

    sibling = (rep, me + 1 - 2 * c)
    partner = (1 - rep, me)
    cols = pl.ds(pl.multiple_of(c * COLS, COLS), COLS)
    cols_o = pl.ds(pl.multiple_of((1 - c) * COLS, COLS), COLS)
    rows = pl.ds(pl.multiple_of(c * HALF, HALF), HALF)
    rows_o = pl.ds(pl.multiple_of((1 - c) * HALF, HALF), HALF)

    def remote(src, dst, send, recv, where):
        return pltpu.make_async_remote_copy(
            src_ref=src, dst_ref=dst, send_sem=send, recv_sem=recv, device_id=where, device_id_type=MESH
        )

    local = [
        pltpu.make_async_copy(w_in.at[0, :, cols], wv.at[rows], loc_sem.at[0]),
        pltpu.make_async_copy(m_in.at[0, :, cols], mv.at[rows], loc_sem.at[1]),
        pltpu.make_async_copy(v_in.at[0, :, cols], vv.at[rows], loc_sem.at[2]),
        pltpu.make_async_copy(gw_in, gl.at[0], loc_sem.at[3]),
        pltpu.make_async_copy(om_in, gl.at[1], loc_sem.at[4]),
        pltpu.make_async_copy(og_in.at[0], og.at[0], loc_sem.at[5]),
    ]
    for copy in local:
        copy.start()

    barrier = pltpu.get_barrier_semaphore()
    peers = [(dx, 0, dz) for dx in range(4) for dz in range(2) if dx or dz]
    peers += [(0, dy, dz) for dy in range(1, 4) for dz in range(2)]
    partners = [dev(*p) for p in peers] + [sibling, partner]
    for where in partners:
        pl.semaphore_signal(barrier, inc=1, device_id=where, device_id_type=MESH)
    pl.semaphore_wait(barrier, len(partners))

    pre = [
        remote(w_in.at[0, :, cols_o], wv.at[rows], pre_send.at[0], pre_recv.at[0], sibling),
        remote(m_in.at[0, :, cols_o], mv.at[rows], pre_send.at[1], pre_recv.at[1], sibling),
        remote(v_in.at[0, :, cols_o], vv.at[rows], pre_send.at[2], pre_recv.at[2], sibling),
        remote(og_in.at[0], og.at[1], pre_send.at[3], pre_recv.at[3], partner),
    ]
    for copy in pre:
        copy.start()

    def x_copies(step):
        own = pl.ds(0, LOCAL)
        other = pl.ds(LOCAL, LOCAL)
        return [
            pltpu.make_async_copy(x_in.at[0, step], xv.at[step, own], x_loc.at[step, 0]),
            pltpu.make_async_copy(t_in.at[0, step, :, cols], tv.at[step, own], x_loc.at[step, 1]),
            remote(x_in.at[0, step], xv.at[step, other], x_send.at[step, 0], x_recv.at[step, 0], sibling),
            remote(t_in.at[0, step, :, cols_o], tv.at[step, other], x_send.at[step, 1], x_recv.at[step, 1], sibling),
        ]

    for copy in x_copies(0):
        copy.start()
    local[0].wait()
    pre[0].wait_recv()

    def own_rows(kind):
        return slice(0, HALF) if kind == 0 else slice(HALF, ROWS)

    def delta(kind, along, dz):
        return (along, 0, dz) if kind == 0 else (0, along, dz)

    def long_delta(kind, along):
        return (0, along, 0) if kind == 0 else (along, 0, 0)

    def slot(along, dz):
        return dz * 4 + along

    def back(along):
        return (4 - along) % 4

    def gather_one(k, kind, along, dz):
        piece = wg.at[k, x, y, zh, own_rows(kind)]
        return remote(
            piece,
            piece,
            a1_send.at[k, kind, slot(along, dz)],
            a1_recv.at[k, kind, slot(back(along), dz)],
            dev(*delta(kind, along, dz)),
        )

    def gather_two(k, kind, plane, along):
        nz = 1 - zh if plane else zh
        lane = wg.at[k, :, y, nz, own_rows(kind)] if kind == 0 else wg.at[k, x, :, nz, own_rows(kind)]
        return remote(
            lane,
            lane,
            a2_send.at[k, kind, plane, along],
            a2_recv.at[k, kind, plane, back(along)],
            dev(*long_delta(kind, along)),
        )

    def scatter_two(k, kind, along):
        if kind == 0:
            src = gb.at[k, :, lax.rem(y + along, 4), :, 0:CH]
        else:
            src = gb.at[k, lax.rem(x + along, 4), :, :, CH:CK]
        return remote(
            src,
            r2.at[k, kind, back(along) - 1],
            r2_send.at[k, kind, along],
            r2_recv.at[k, kind, back(along)],
            dev(*long_delta(kind, along)),
        )

    def scatter_one(k, kind, along, dz):
        return remote(
            s1.at[k, kind, slot(along, dz)],
            r1.at[k, kind, slot(back(along), dz)],
            r1_send.at[k, kind, slot(along, dz)],
            r1_recv.at[k, kind, slot(back(along), dz)],
            dev(*delta(kind, along, dz)),
        )

    longs = (2, 1, 3)
    short = [(along, dz) for dz in range(2) for along in (2, 1, 3, 0) if along or dz]

    def gather_start(k):
        wg[k, x, y, zh] = wv[:, k * CK : (k + 1) * CK].astype(BF16)
        for along, dz in short:
            for kind in range(2):
                gather_one(k, kind, along, dz).start()

    def gather_forward(k, plane):
        for kind in range(2):
            for along, dz in short:
                if dz == plane:
                    gather_one(k, kind, along, dz).wait_recv()
            for along in longs:
                gather_two(k, kind, plane, along).start()

    def gather_end(k):
        for plane in range(2):
            for kind in range(2):
                for along in longs:
                    gather_two(k, kind, plane, along).wait_recv()

    def gather_drain(k):
        for kind in range(2):
            for along, dz in short:
                gather_one(k, kind, along, dz).wait_send()
            for plane in range(2):
                for along in longs:
                    gather_two(k, kind, plane, along).wait_send()

    def outer():
        for copy in local[1:]:
            copy.wait()
        for copy in pre[1:]:
            copy.wait_recv()
        mean = (og[0].astype(F32) + og[1].astype(F32)) / 2.0
        momentum = 0.9 * gl[1] + mean
        gl[1] = momentum
        gl[0] = gl[0] - 0.7 * (mean + 0.9 * momentum)
        here = pltpu.make_async_copy(gl.at[0, :, cols], gv.at[rows], loc_sem.at[6])
        there = remote(gl.at[0, :, cols_o], gv.at[rows], pre_send.at[4], pre_recv.at[4], sibling)
        outs = [
            pltpu.make_async_copy(gl.at[0], g_out, out_loc.at[0]),
            pltpu.make_async_copy(gl.at[1], mo_out, out_loc.at[1]),
        ]
        for copy in [here, there] + outs:
            copy.start()
        here.wait()
        there.wait()
        for copy in outs:
            copy.wait()
        for copy in pre:
            copy.wait_send()

    def forward(k, step, first, last):
        def block_of(i, carry):
            block = pl.ds(pl.multiple_of(i * 512, 512), 512)
            product = dot(xv[step, block, :], wg[k].reshape(D, CK))
            residual = product * inv_root - tv[step, block, k * CK : (k + 1) * CK].astype(F32)
            rt[:, block] = residual.astype(BF16).T
            return carry

        lax.fori_loop(first, last, block_of, 0)

    def backward(k, step):
        for tiles, send in GROUPS:
            for dx, dy in tiles:
                nx, ny = lax.rem(x + dx, 4), lax.rem(y + dy, 4)
                lanes = pl.ds(pl.multiple_of((nx * 4 + ny) * 256, 256), 256)
                tile = dot(rt[...], xv[step, :, lanes]).astype(BF16)
                gb[k, nx, ny, 0] = tile[:, :ROWS]
                gb[k, nx, ny, 1] = tile[:, ROWS:]
            if send is not None:
                scatter_two(k, *send).start()

    def add_long(k):
        for kind in range(2):
            for along in longs:
                scatter_two(k, kind, along).wait_recv()
            mine = slice(0, CH) if kind == 0 else slice(CH, CK)
            for along, dz in short + [(0, 0)]:
                nz = 1 - zh if dz else zh
                far = lax.rem((x if kind == 0 else y) + along, 4)
                here = gb[k, far, y, nz, mine] if kind == 0 else gb[k, x, far, nz, mine]
                total = here.astype(F32)
                for source in range(3):
                    total += r2[k, kind, source, far, nz].astype(F32)
                if along or dz:
                    s1[k, kind, slot(along, dz)] = total.astype(BF16)
                    scatter_one(k, kind, along, dz).start()
                else:
                    kept[k, kind] = total

    def update(k, step):
        halves = []
        for kind in range(2):
            total = kept[k, kind]
            for along, dz in short:
                scatter_one(k, kind, along, dz).wait_recv()
                total += r1[k, kind, slot(back(along), dz)].astype(F32)
            halves.append(total)
        gradient = jnp.concatenate(halves, axis=0).T * inv_root
        part = slice(k * CK, (k + 1) * CK)
        first = 0.9 * mv[:, part] + 0.1 * gradient
        second = 0.95 * vv[:, part] + 0.05 * gradient * gradient
        weight = wv[:, part]
        weight = weight - 0.05 * (first / (jnp.sqrt(second) + 1e-08) + 0.1 * weight)
        weight = jnp.where(sync_in[0] == step, 0.5 * weight + 0.5 * gv[:, part], weight)
        mv[:, part] = first
        vv[:, part] = second
        wv[:, part] = weight

    def scatter_drain(k):
        for kind in range(2):
            for along in longs:
                scatter_two(k, kind, along).wait_send()
            for along, dz in short:
                scatter_one(k, kind, along, dz).wait_send()

    def results(k):
        ends = []
        part = pl.ds(pl.multiple_of(c * COLS + k * CK, CK), CK)
        for i, (value, out) in enumerate(((wv, w_out), (mv, m_out), (vv, v_out))):
            mine = pl.ds(k * CK, CK)
            ends.append(
                remote(value.at[rows_o, mine], out.at[0, :, part], out_send.at[k, i], out_recv.at[k, i], sibling)
            )
            ends.append(pltpu.make_async_copy(value.at[rows, mine], out.at[0, :, part], out_loc.at[2 + 3 * k + i]))
        return ends

    gather_start(0)

    def inner(step, carry):
        gather_forward(0, 0)
        gather_forward(0, 1)

        @pl.when(step > 0)
        def late():
            update(1, step - 1)

        gather_start(1)

        @pl.when(step > 0)
        def clear():
            scatter_drain(1)

        gather_forward(1, 0)

        @pl.when(step == 0)
        def once():
            outer()

        gather_end(0)
        for copy in x_copies(step):
            copy.wait()

        @pl.when(step == 0)
        def more():
            for copy in x_copies(1):
                copy.start()

        forward(0, step, 0, 2)
        gather_forward(1, 1)
        forward(0, step, 2, 4)
        gather_drain(0)
        backward(0, step)
        gather_end(1)
        forward(1, step, 0, 4)
        gather_drain(1)
        backward(1, step)
        add_long(0)
        update(0, step)

        @pl.when(step < STEPS - 1)
        def again():
            gather_start(0)

        scatter_drain(0)
        add_long(1)
        return carry

    lax.fori_loop(0, STEPS, inner, 0)

    early = results(0)
    for copy in early:
        copy.start()
    update(1, STEPS - 1)
    ends = results(1)
    for copy in ends:
        copy.start()
    scatter_drain(1)
    for copy in early + ends:
        copy.wait()


def settle(*refs):
    ins, outs, sems = refs[:5], refs[5:10], refs[10]
    copies = [pltpu.make_async_copy(a, b, sems.at[i]) for i, (a, b) in enumerate(zip(ins, outs))]
    for copy in copies:
        copy.start()
    for copy in copies:
        copy.wait()


def per_device(*args):
    shapes = ((1, 64, KVW),) * 3 + ((64, KVW),) * 2
    dma = pltpu.SemaphoreType.DMA
    anywhere = pl.BlockSpec(memory_space=pl.ANY)
    out_shape = tuple(jax.ShapeDtypeStruct(s, F32) for s in shapes)
    values = pl.pallas_call(
        kernel,
        out_shape=out_shape,
        in_specs=[anywhere] * 8 + [pl.BlockSpec(memory_space=pltpu.SMEM)],
        out_specs=(anywhere,) * 5,
        scratch_shapes=[
            pltpu.VMEM((STEPS, TOK, D), BF16),
            pltpu.VMEM((STEPS, TOK, COLS), BF16),
            pltpu.VMEM((ROWS, COLS), F32),
            pltpu.VMEM((ROWS, COLS), F32),
            pltpu.VMEM((ROWS, COLS), F32),
            pltpu.VMEM((ROWS, COLS), F32),
            pltpu.VMEM((2, HALF, KVW), F32),
            pltpu.VMEM((2, HALF, KVW), BF16),
            pltpu.VMEM((CHUNKS, NX, NY, NZ, ROWS, CK), BF16),
            pltpu.VMEM((CK, TOK), BF16),
            pltpu.VMEM((CHUNKS, NX, NY, NZ, CK, ROWS), BF16),
            pltpu.VMEM((CHUNKS, 2, 3, 4, NZ, CH, ROWS), BF16),
            pltpu.VMEM((CHUNKS, 2, 8, CH, ROWS), BF16),
            pltpu.VMEM((CHUNKS, 2, 8, CH, ROWS), BF16),
            pltpu.VMEM((CHUNKS, 2, CH, ROWS), F32),
            dma((7,)),
            dma((5,)),
            dma((5,)),
            dma((STEPS, 2)),
            dma((STEPS, 2)),
            dma((STEPS, 2)),
            dma((CHUNKS, 2, 8)),
            dma((CHUNKS, 2, 8)),
            dma((CHUNKS, 2, 2, 4)),
            dma((CHUNKS, 2, 2, 4)),
            dma((CHUNKS, 2, 4)),
            dma((CHUNKS, 2, 4)),
            dma((CHUNKS, 2, 8)),
            dma((CHUNKS, 2, 8)),
            dma((2 + 3 * CHUNKS,)),
            dma((CHUNKS, 3)),
            dma((CHUNKS, 3)),
        ],
        compiler_params=pltpu.CompilerParams(
            collective_id=0, has_side_effects=True, vmem_limit_bytes=60 * 1024 * 1024
        ),
    )(*args)
    return pl.pallas_call(
        settle,
        out_shape=out_shape,
        in_specs=[anywhere] * 5,
        out_specs=(anywhere,) * 5,
        scratch_shapes=[dma((5,))],
    )(*values)


def solution(mesh):
    in_specs = (
        P("replica", None, "fsdp", None),
        P("replica", None, "fsdp", None),
        P("replica", "fsdp", None),
        P("replica", "fsdp", None),
        P("replica", "fsdp", None),
        P("fsdp", None),
        P("fsdp", None),
        P("replica", "fsdp", None),
        P(),
    )
    out_specs = (
        P("replica", "fsdp", None),
        P("replica", "fsdp", None),
        P("replica", "fsdp", None),
        P("fsdp", None),
        P("fsdp", None),
    )
    return jax.shard_map(
        per_device, mesh=mesh, in_specs=in_specs, out_specs=out_specs, check_vma=False
    )
```

time: 123 us -> 123 us (level)
  Pallas kernels: 113 us -> 122 us
  local copies, waits for them, and re-layouts: 7.84 us -> 0 us
    pallas_call x1 -> x2, Pallas kernels: 113 us -> 122 us  [the longest x1 101 us: per_device(): pl.pallas_call(kernel, out_shape=out_shape, in_specs=[anywhere] * 8 + [pl...]
    unnamed x5 -> x0, local copies, waits for them, and re-layouts: 7.84 us -> none
where the time goes in v2:
time: 123 us
  Pallas kernels  122 us (99%)
  between operations  1.29 us (1%)
    pallas_call x1, Pallas kernels, per_device(): pl.pallas_call(kernel, out_shape=out_shape, in_specs=[anywhere] * 8 + [pl...  101 us
    pallas_call x1, Pallas kernels, per_device(): pl.pallas_call(settle, out_shape=out_shape, in_specs=[anywhere] * 5, out_...  21 us

profile of v2, /device:TPU:1, one launch (start us, length us, event | category | flops | bytes accessed | tf_op | source)
XLA Modules:
  0.0 123.0 jit_solution(13927649874447741035)
XLA Ops:
  1.3 100.7 %shard_map.128 = (f32[1,64,512]{2,1,0:T(8,128)}, f32[1,64,512]{2,1,0:T(8,128)}, f32[1,64,512]{2,1,0:T(8,128)}, f32[64,512]{1,0:T(8,128)}, f32[64,512]{1,0:T(8,128)}) custom-call(bf16[1,2,1024,4096]{3,2,1,0:T(8,128)(2,1)} %x_in.1, bf16[1,2,1024,512]{3,2,1,0:T(8,128)(2,1)} %t_in.1, f32[1,64,512]{2,1,0:T(8,128)} %w_in.1, f32[1,64,512]{2,1,0:T(8,128)} %m_in.1, ...), custom_call_target="tpu_custom_call" | custom-call | tf_op jit(solution)/shard_map/pallas_call | solution.py:426
  102.0 21.0 %shard_map.129 = (f32[1,64,512]{2,1,0:T(8,128)}, f32[1,64,512]{2,1,0:T(8,128)}, f32[1,64,512]{2,1,0:T(8,128)}, f32[64,512]{1,0:T(8,128)}, f32[64,512]{1,0:T(8,128)}) custom-call(f32[1,64,512]{2,1,0:T(8,128)} %get-tuple-element.10.refs_0_, f32[1,64,512]{2,1,0:T(8,128)} %get-tuple-element.11.refs_1_, f32[1,64,512]{2,1,0:T(8,128)} %get-tuple-element.12.refs_2_, ...), custom_call_target="tpu_custom_call" | custom-call | tf_op jit(solution)/shard_map/pallas_call | solution.py:469

commit v3 on v1

v3 whole, which is shorter than its diff:
```python
import functools
import math

import jax
import jax.numpy as jnp
from jax import lax
from jax.experimental import pallas as pl
from jax.experimental.pallas import tpu as pltpu
from jax.sharding import PartitionSpec as P

D = 4096
KVW = 512
STEPS = 2
NX, NY, NZ = 4, 4, 2
LOCAL = 1024
TOK = 2 * LOCAL
COLS = KVW // 2
ROWS = 128
HALF = ROWS // 2
CH = COLS // 2
MESH = pl.DeviceIdType.MESH
F32 = jnp.float32
BF16 = jnp.bfloat16

TILES = (
    ((2, 1), (2, 2), (2, 3), (1, 2), (3, 2))
    + ((1, 1), (1, 3), (3, 1), (3, 3))
    + ((0, 2), (2, 0), (0, 1), (1, 0), (0, 3), (3, 0), (0, 0))
)


def dot(a, b):
    return lax.dot_general(a, b, (((1,), (0,)), ((), ())), preferred_element_type=F32)


def kernel(
    x_in,
    t_in,
    w_in,
    m_in,
    v_in,
    gw_in,
    om_in,
    og_in,
    sync_in,
    w_out,
    m_out,
    v_out,
    g_out,
    mo_out,
    xv,
    tv,
    wv,
    mv,
    vv,
    gv,
    gl,
    og,
    wg,
    pt,
    rt,
    gb,
    r2,
    s1,
    r1,
    kept,
    loc_sem,
    pre_send,
    pre_recv,
    x_loc,
    x_send,
    x_recv,
    gz_send,
    gz_recv,
    g1_send,
    g1_recv,
    g2_send,
    g2_recv,
    r2_send,
    r2_recv,
    r1_send,
    r1_recv,
    out_loc,
    out_send,
    out_recv,
):
    inv_root = 1.0 / math.sqrt(D)
    rep = lax.axis_index("replica")
    me = lax.axis_index("fsdp")
    c = lax.rem(me, 2)
    zh = lax.rem(lax.div(me, 2), 2)
    y = lax.rem(lax.div(me, 4), 4)
    x = lax.div(me, 16)

    def dev(dx, dy, dz):
        nx, ny = lax.rem(x + dx, 4), lax.rem(y + dy, 4)
        nz = 1 - zh if dz else zh
        return (rep, ((nx * 4 + ny) * 2 + nz) * 2 + c)

    sibling = (rep, me + 1 - 2 * c)
    partner = (1 - rep, me)
    cols = pl.ds(pl.multiple_of(c * COLS, COLS), COLS)
    cols_o = pl.ds(pl.multiple_of((1 - c) * COLS, COLS), COLS)
    rows = pl.ds(pl.multiple_of(c * HALF, HALF), HALF)
    rows_o = pl.ds(pl.multiple_of((1 - c) * HALF, HALF), HALF)

    def remote(src, dst, send, recv, where):
        return pltpu.make_async_remote_copy(
            src_ref=src, dst_ref=dst, send_sem=send, recv_sem=recv, device_id=where, device_id_type=MESH
        )

    local = [
        pltpu.make_async_copy(w_in.at[0, :, cols], wv.at[rows], loc_sem.at[0]),
        pltpu.make_async_copy(m_in.at[0, :, cols], mv.at[rows], loc_sem.at[1]),
        pltpu.make_async_copy(v_in.at[0, :, cols], vv.at[rows], loc_sem.at[2]),
        pltpu.make_async_copy(gw_in, gl.at[0], loc_sem.at[3]),
        pltpu.make_async_copy(om_in, gl.at[1], loc_sem.at[4]),
        pltpu.make_async_copy(og_in.at[0], og.at[0], loc_sem.at[5]),
    ]
    for copy in local:
        copy.start()

    barrier = pltpu.get_barrier_semaphore()
    peers = [(dx, 0, dz) for dx in range(4) for dz in range(2) if dx or dz]
    peers += [(0, dy, dz) for dy in range(1, 4) for dz in range(2)]
    partners = [dev(*p) for p in peers] + [sibling, partner]
    for where in partners:
        pl.semaphore_signal(barrier, inc=1, device_id=where, device_id_type=MESH)
    pl.semaphore_wait(barrier, len(partners))

    pre = [
        remote(w_in.at[0, :, cols_o], wv.at[rows], pre_send.at[0], pre_recv.at[0], sibling),
        remote(m_in.at[0, :, cols_o], mv.at[rows], pre_send.at[1], pre_recv.at[1], sibling),
        remote(v_in.at[0, :, cols_o], vv.at[rows], pre_send.at[2], pre_recv.at[2], sibling),
        remote(og_in.at[0], og.at[1], pre_send.at[3], pre_recv.at[3], partner),
    ]
    for copy in pre:
        copy.start()

    def x_copies(step):
        own = pl.ds(0, LOCAL)
        other = pl.ds(LOCAL, LOCAL)
        return [
            pltpu.make_async_copy(x_in.at[0, step], xv.at[step, own], x_loc.at[step, 0]),
            pltpu.make_async_copy(t_in.at[0, step, :, cols], tv.at[step, own], x_loc.at[step, 1]),
            remote(x_in.at[0, step], xv.at[step, other], x_send.at[step, 0], x_recv.at[step, 0], sibling),
            remote(t_in.at[0, step, :, cols_o], tv.at[step, other], x_send.at[step, 1], x_recv.at[step, 1], sibling),
        ]

    for copy in x_copies(0):
        copy.start()
    local[0].wait()
    pre[0].wait_recv()

    def half(kind):
        return slice(0, HALF) if kind == 0 else slice(HALF, ROWS)

    def long_delta(kind, along):
        return (0, along, 0) if kind == 0 else (along, 0, 0)

    def short_delta(kind, along, dz):
        return (along, 0, dz) if kind == 0 else (0, along, dz)

    def slot(along, dz):
        return dz * 4 + along

    def back(along):
        return (4 - along) % 4

    def plane_z(plane):
        return 1 - zh if plane else zh

    def gather_z():
        piece = wg.at[x, y, zh]
        return remote(piece, piece, gz_send.at[0], gz_recv.at[0], dev(0, 0, 1))

    def gather_ring(plane, axis, along):
        piece = wg.at[x, y, plane_z(plane)]
        return remote(
            piece,
            piece,
            g1_send.at[plane, axis, along],
            g1_recv.at[plane, axis, back(along)],
            dev(*((along, 0, 0) if axis == 0 else (0, along, 0))),
        )

    def gather_long(plane, kind, along, rel):
        nz = plane_z(plane)
        if kind == 0:
            piece = wg.at[lax.rem(x + rel, 4), y, nz, half(0)]
        else:
            piece = wg.at[x, lax.rem(y + rel, 4), nz, half(1)]
        return remote(
            piece,
            piece,
            g2_send.at[plane, kind, along, rel],
            g2_recv.at[plane, kind, back(along), rel],
            dev(*long_delta(kind, along)),
        )

    def scatter_long(kind, along, rel):
        if kind == 0:
            src = gb.at[lax.rem(x + rel, 4), lax.rem(y + along, 4), :, 0:CH]
        else:
            src = gb.at[lax.rem(x + along, 4), lax.rem(y + rel, 4), :, CH:COLS]
        return remote(
            src,
            r2.at[kind, back(along) - 1, rel],
            r2_send.at[kind, along, rel],
            r2_recv.at[kind, back(along), rel],
            dev(*long_delta(kind, along)),
        )

    def scatter_short(kind, along, dz):
        return remote(
            s1.at[kind, slot(along, dz)],
            r1.at[kind, slot(back(along), dz)],
            r1_send.at[kind, slot(along, dz)],
            r1_recv.at[kind, slot(back(along), dz)],
            dev(*short_delta(kind, along, dz)),
        )

    others = (1, 3, 2)
    short = [(along, dz) for dz in range(2) for along in (2, 1, 3, 0) if along or dz]

    def gather_start():
        wg[x, y, zh] = wv[...].astype(BF16)
        gather_z().start()
        for along in others:
            for axis in range(2):
                gather_ring(0, axis, along).start()

    def gather_forward(plane):
        for rel in others:
            for kind in range(2):
                gather_ring(plane, kind, back(rel)).wait_recv()
                for along in others:
                    gather_long(plane, kind, along, rel).start()

    def gather_turn():
        gather_z().wait_recv()
        for along in others:
            for axis in range(2):
                gather_ring(1, axis, along).start()

    def gather_end(plane):
        for kind in range(2):
            for along in others:
                for rel in others:
                    gather_long(plane, kind, along, rel).wait_recv()

    def gather_drain():
        gather_z().wait_send()
        for plane in range(2):
            for kind in range(2):
                for along in others:
                    gather_ring(plane, kind, along).wait_send()
                    for rel in others:
                        gather_long(plane, kind, along, rel).wait_send()

    def outer_ends():
        here = pltpu.make_async_copy(gl.at[0, :, cols], gv.at[rows], loc_sem.at[6])
        there = remote(gl.at[0, :, cols_o], gv.at[rows], pre_send.at[4], pre_recv.at[4], sibling)
        outs = [
            pltpu.make_async_copy(gl.at[0], g_out, out_loc.at[0]),
            pltpu.make_async_copy(gl.at[1], mo_out, out_loc.at[1]),
        ]
        return [here, there] + outs

    def outer():
        for copy in local[1:]:
            copy.wait()
        for copy in pre[1:]:
            copy.wait_recv()
        mean = (og[0].astype(F32) + og[1].astype(F32)) / 2.0
        momentum = 0.9 * gl[1] + mean
        gl[1] = momentum
        gl[0] = gl[0] - 0.7 * (mean + 0.9 * momentum)
        for copy in outer_ends():
            copy.start()

    def forward(plane, step):
        nz = plane_z(plane)

        def block_of(i, carry):
            block = pl.ds(pl.multiple_of(i * 512, 512), 512)
            strips = [
                xv[step, block, pl.ds(pl.multiple_of(k * 256 + nz * ROWS, ROWS), ROWS)] for k in range(NX * NY)
            ]
            part = dot(jnp.concatenate(strips, axis=1), wg[:, :, nz].reshape(NX * NY * ROWS, COLS))
            if plane == 0:
                pt[block, :] = part
            else:
                product = pt[block, :] + part
                residual = product * inv_root - tv[step, block, :].astype(F32)
                rt[:, block] = residual.astype(BF16).T
            return carry

        lax.fori_loop(0, TOK // 512, block_of, 0)

    def backward(step):
        for dx, dy in TILES:
            nx, ny = lax.rem(x + dx, 4), lax.rem(y + dy, 4)
            lanes = pl.ds(pl.multiple_of((nx * 4 + ny) * 256, 256), 256)
            tile = dot(rt[...], xv[step, :, lanes]).astype(BF16)
            gb[nx, ny, 0] = tile[:, :ROWS]
            gb[nx, ny, 1] = tile[:, ROWS:]
            if dy:
                scatter_long(0, dy, dx).start()
            if dx:
                scatter_long(1, dx, dy).start()

    def add_long():
        for rel in (2, 1, 3, 0):
            for kind in range(2):
                for along in others:
                    scatter_long(kind, along, rel).wait_recv()
                mine = slice(0, CH) if kind == 0 else slice(CH, COLS)
                far = lax.rem((x if kind == 0 else y) + rel, 4)
                for dz in (1, 0):
                    nz = plane_z(dz)
                    here = gb[far, y, nz, mine] if kind == 0 else gb[x, far, nz, mine]
                    total = here.astype(F32)
                    for source in range(3):
                        total += r2[kind, source, rel, nz].astype(F32)
                    if rel or dz:
                        s1[kind, slot(rel, dz)] = total.astype(BF16)
                        scatter_short(kind, rel, dz).start()
                    else:
                        kept[kind] = total

    def update(step):
        halves = []
        for kind in range(2):
            total = kept[kind]
            for along, dz in short:
                scatter_short(kind, along, dz).wait_recv()
                total += r1[kind, slot(back(along), dz)].astype(F32)
            halves.append(total)
        gradient = jnp.concatenate(halves, axis=0).T * inv_root
        first = 0.9 * mv[...] + 0.1 * gradient
        second = 0.95 * vv[...] + 0.05 * gradient * gradient
        weight = wv[...]
        weight = weight - 0.05 * (first / (jnp.sqrt(second) + 1e-08) + 0.1 * weight)
        weight = jnp.where(sync_in[0] == step, 0.5 * weight + 0.5 * gv[...], weight)
        mv[...] = first
        vv[...] = second
        wv[...] = weight

    def scatter_drain():
        for kind in range(2):
            for along in others:
                for rel in range(4):
                    scatter_long(kind, along, rel).wait_send()
            for along, dz in short:
                scatter_short(kind, along, dz).wait_send()

    gather_start()

    def inner(step, carry):
        gather_turn()
        gather_forward(0)

        @pl.when(step == 0)
        def once():
            outer()

        gather_forward(1)
        gather_end(0)
        for copy in x_copies(step):
            copy.wait()

        @pl.when(step == 0)
        def more():
            for copy in x_copies(1):
                copy.start()
            for copy in outer_ends():
                copy.wait()
            for copy in pre:
                copy.wait_send()

        forward(0, step)
        gather_end(1)
        forward(1, step)
        gather_drain()
        backward(step)
        add_long()
        update(step)

        @pl.when(step < STEPS - 1)
        def again():
            gather_start()

        scatter_drain()
        return carry

    lax.fori_loop(0, STEPS, inner, 0)

    ends = []
    for i, (value, out) in enumerate(((wv, w_out), (mv, m_out), (vv, v_out))):
        ends.append(remote(value.at[rows_o], out.at[0, :, cols], out_send.at[i], out_recv.at[i], sibling))
        ends.append(pltpu.make_async_copy(value.at[rows], out.at[0, :, cols], out_loc.at[2 + i]))
    for copy in ends:
        copy.start()
    for copy in ends:
        copy.wait()


def settle(*refs):
    ins, outs, sems = refs[:5], refs[5:10], refs[10]
    copies = [pltpu.make_async_copy(a, b, sems.at[i]) for i, (a, b) in enumerate(zip(ins, outs))]
    for copy in copies:
        copy.start()
    for copy in copies:
        copy.wait()


def per_device(*args):
    shapes = ((1, 64, KVW),) * 3 + ((64, KVW),) * 2
    dma = pltpu.SemaphoreType.DMA
    anywhere = pl.BlockSpec(memory_space=pl.ANY)
    out_shape = tuple(jax.ShapeDtypeStruct(s, F32) for s in shapes)
    values = pl.pallas_call(
        kernel,
        out_shape=out_shape,
        in_specs=[anywhere] * 8 + [pl.BlockSpec(memory_space=pltpu.SMEM)],
        out_specs=(anywhere,) * 5,
        scratch_shapes=[
            pltpu.VMEM((STEPS, TOK, D), BF16),
            pltpu.VMEM((STEPS, TOK, COLS), BF16),
            pltpu.VMEM((ROWS, COLS), F32),
            pltpu.VMEM((ROWS, COLS), F32),
            pltpu.VMEM((ROWS, COLS), F32),
            pltpu.VMEM((ROWS, COLS), F32),
            pltpu.VMEM((2, HALF, KVW), F32),
            pltpu.VMEM((2, HALF, KVW), BF16),
            pltpu.VMEM((NX, NY, NZ, ROWS, COLS), BF16),
            pltpu.VMEM((TOK, COLS), F32),
            pltpu.VMEM((COLS, TOK), BF16),
            pltpu.VMEM((NX, NY, NZ, COLS, ROWS), BF16),
            pltpu.VMEM((2, 3, 4, NZ, CH, ROWS), BF16),
            pltpu.VMEM((2, 8, CH, ROWS), BF16),
            pltpu.VMEM((2, 8, CH, ROWS), BF16),
            pltpu.VMEM((2, CH, ROWS), F32),
            dma((7,)),
            dma((5,)),
            dma((5,)),
            dma((STEPS, 2)),
            dma((STEPS, 2)),
            dma((STEPS, 2)),
            dma((1,)),
            dma((1,)),
            dma((2, 2, 4)),
            dma((2, 2, 4)),
            dma((2, 2, 4, 4)),
            dma((2, 2, 4, 4)),
            dma((2, 4, 4)),
            dma((2, 4, 4)),
            dma((2, 8)),
            dma((2, 8)),
            dma((5,)),
            dma((3,)),
            dma((3,)),
        ],
        compiler_params=pltpu.CompilerParams(
            collective_id=0, has_side_effects=True, vmem_limit_bytes=60 * 1024 * 1024
        ),
    )(*args)
    return pl.pallas_call(
        settle,
        out_shape=out_shape,
        in_specs=[anywhere] * 5,
        out_specs=(pl.BlockSpec(memory_space=pltpu.VMEM),) * 5,
        scratch_shapes=[dma((5,))],
    )(*values)


def solution(mesh):
    in_specs = (
        P("replica", None, "fsdp", None),
        P("replica", None, "fsdp", None),
        P("replica", "fsdp", None),
        P("replica", "fsdp", None),
        P("replica", "fsdp", None),
        P("fsdp", None),
        P("fsdp", None),
        P("replica", "fsdp", None),
        P(),
    )
    out_specs = (
        P("replica", "fsdp", None),
        P("replica", "fsdp", None),
        P("replica", "fsdp", None),
        P("fsdp", None),
        P("fsdp", None),
    )
    return jax.shard_map(
        per_device, mesh=mesh, in_specs=in_specs, out_specs=out_specs, check_vma=False
    )
```

time: 123 us -> 99.9 us (0.81)
  Pallas kernels: 113 us -> 98.4 us
  local copies, waits for them, and re-layouts: 7.84 us -> 0 us
    pallas_call x1 -> x2, Pallas kernels: 113 us -> 98.4 us  [the longest x1 96.4 us: per_device(): pl.pallas_call(kernel, out_shape=out_shape, in_specs=[anywhere] * 8 + [pl...]
    unnamed x5 -> x0, local copies, waits for them, and re-layouts: 7.84 us -> none
where the time goes in v3:
time: 99.9 us; the launch traced here: 99.7 us
  Pallas kernels  98.4 us (98%)
  between operations  1.29 us (1%)
    pallas_call x1, Pallas kernels, per_device(): pl.pallas_call(kernel, out_shape=out_shape, in_specs=[anywhere] * 8 + [pl...  96.4 us
    pallas_call x1, Pallas kernels, per_device(): pl.pallas_call(settle, out_shape=out_shape, in_specs=[anywhere] * 5, out_...  2.04 us

profile of v3, /device:TPU:1, one launch (start us, length us, event | category | flops | bytes accessed | tf_op | source)
XLA Modules:
  0.0 99.7 jit_solution(4666837399751850553)
XLA Ops:
  1.3 96.4 %shard_map.128 = (f32[1,64,512]{2,1,0:T(8,128)}, f32[1,64,512]{2,1,0:T(8,128)}, f32[1,64,512]{2,1,0:T(8,128)}, f32[64,512]{1,0:T(8,128)}, f32[64,512]{1,0:T(8,128)}) custom-call(bf16[1,2,1024,4096]{3,2,1,0:T(8,128)(2,1)} %x_in.1, bf16[1,2,1024,512]{3,2,1,0:T(8,128)(2,1)} %t_in.1, f32[1,64,512]{2,1,0:T(8,128)} %w_in.1, f32[1,64,512]{2,1,0:T(8,128)} %m_in.1, ...), custom_call_target="tpu_custom_call" | custom-call | tf_op jit(solution)/shard_map/pallas_call | solution.py:423
  97.7 2.0 %shard_map.129 = (f32[1,64,512]{2,1,0:T(8,128)}, f32[1,64,512]{2,1,0:T(8,128)}, f32[1,64,512]{2,1,0:T(8,128)}, f32[64,512]{1,0:T(8,128)}, f32[64,512]{1,0:T(8,128)}) custom-call(f32[1,64,512]{2,1,0:T(8,128)} %get-tuple-element.10.refs_0_, f32[1,64,512]{2,1,0:T(8,128)} %get-tuple-element.11.refs_1_, f32[1,64,512]{2,1,0:T(8,128)} %get-tuple-element.12.refs_2_, ...), custom_call_target="tpu_custom_call" | custom-call | tf_op jit(solution)/shard_map/pallas_call | solution.py:469
